TPU v7x, 128 devices: a whole 4x4x4 slice. The times are simulated.
128 devices in a mesh: row: 16 (over x, z_hi, core), col: 8 (over y, z_lo).
Axes of the slice: x: 4, y: 4, z: 4 (z_hi: 2, z_lo: 2; z = z_hi * 2 + z_lo), core: 2. Of those that a mesh axis runs over, the one named last changes fastest.
Arguments:
- front: float32 [48, 16, 128, 2, 8, 128], P(None, 'row', None, None, 'col')
- child_tiles: float32 [16, 8, 128, 128, 128], P('row', 'col'), may hold values from -1.5 to 1.5
- child_rows: int32 [16, 8, 128], P('row', 'col'), may hold values from 0 to 767, as said below
- child_cols: int32 [16, 8, 128], P('row', 'col'), may hold values from 0 to 15, as said below
Outputs:
- factored: float32 [48, 16, 128, 2, 8, 128], P(None, 'row', None, None, 'col')
Inputs may be any that keep to these rules, and one draw needn't show every extreme that they name: `child_rows`: parent block row of each child block. The owner of front block (i, j) is device (i mod 16, j mod 8); from one device at most 2 child blocks go to one owner, and some owners receive exactly 2 from every device. `child_cols`: parent block column of each child block, among the 2048 columns held; same owner bound as for child_rows.
All inputs are finite; a program needn't handle non-finite values.
Results may differ from a plain program's by a relative error of at most 0.00005.
Values sent between devices are 32-bit elements; how exact they have to be, the bound alone decides.
No kernel may reach another device: no remote copies, remote signals or barrier semaphores. Data moves between devices by JAX's collectives and lax.ppermute only.
A program may use at most 192 MiB of HBM per device.

v0:
```python
import jax
import jax.numpy as jnp
from jax import lax
from jax.sharding import PartitionSpec as P

CAP = 2


def broadcast(value, axis, source):
    kept = jnp.where(lax.axis_index(axis) == source, value, 0).astype(value.dtype)
    return lax.psum(kept, axis)


def factor_of(corner):
    return jnp.linalg.cholesky(0.5 * (corner + corner.T))


def solve_panel(factor, column):
    row_blocks, tile_size = (column.shape[0], column.shape[1])
    flattened = column.reshape(-1, tile_size)
    solved = jax.scipy.linalg.solve_triangular(factor, flattened.T, lower=True).T
    return solved.reshape(row_blocks, tile_size, tile_size)


def per_device(front, child_tiles, child_rows, child_cols):
    row_count = lax.axis_size("row")
    col_count = lax.axis_size("col")
    row_index = lax.axis_index("row")
    col_index = lax.axis_index("col")
    row_blocks, tile_size, col_blocks = (front.shape[0], front.shape[2], front.shape[3])
    local_front = front.reshape(row_blocks, tile_size, col_blocks, tile_size)
    flat_tiles = child_tiles.reshape(-1, tile_size, tile_size)
    parent_rows = child_rows.reshape(-1)
    parent_cols = child_cols.reshape(-1)
    devices = row_count * col_count
    slot_total = devices * CAP
    owners = parent_rows % row_count * col_count + parent_cols % col_count
    one_hot = (owners[:, None] == jnp.arange(devices, dtype=jnp.int32)[None, :]).astype(jnp.int32)
    before = jnp.sum(jnp.cumsum(one_hot, axis=0) * one_hot, axis=1) - 1
    send_slot = owners * CAP + before
    target = parent_rows // row_count * col_blocks + parent_cols // col_count
    send_tiles = (
        jnp.zeros((slot_total, tile_size, tile_size), jnp.float32).at[send_slot].set(flat_tiles)
    )
    send_index = jnp.full((slot_total,), -1, jnp.int32).at[send_slot].set(target)
    arrived_tiles, arrived_index = (
        lax.all_to_all(send_tiles, ("row", "col"), split_axis=0, concat_axis=0, tiled=True),
        lax.all_to_all(send_index, ("row", "col"), split_axis=0, concat_axis=0, tiled=True),
    )
    selector = (
        arrived_index[None, :] == jnp.arange(row_blocks * col_blocks, dtype=jnp.int32)[:, None]
    ).astype(jnp.float32)
    selector = selector.reshape(row_blocks, col_blocks, slot_total)
    assembled = local_front + jnp.einsum(
        "ams,spq->apmq", selector, arrived_tiles, precision=lax.Precision.HIGHEST
    )
    column = assembled[:, :, 0, :]
    corner = broadcast(column[0], "row", 0)
    panel_rows = solve_panel(factor_of(corner), column)
    panel_rows = broadcast(panel_rows, "col", 0)
    window_blocks = col_blocks * col_count // row_count
    window = lax.all_gather(panel_rows[:window_blocks][:, None], "row", axis=1, tiled=True)
    window = window.reshape(col_blocks, col_count, tile_size, tile_size)
    own_window = lax.dynamic_index_in_dim(window, col_index, axis=1, keepdims=False)
    update = jnp.einsum("apk,mqk->apmq", panel_rows, own_window, precision=lax.Precision.HIGHEST)
    global_rows = (jnp.arange(row_blocks, dtype=jnp.int32) * row_count + row_index)[
        :, None, None, None
    ]
    global_cols = (jnp.arange(col_blocks, dtype=jnp.int32) * col_count + col_index)[
        None, None, :, None
    ]
    result = assembled - jnp.where(global_rows > 0, update, jnp.zeros_like(update))
    result = jnp.where(global_cols == 0, panel_rows[:, :, None, :], result)
    return result.reshape(front.shape)


def solution(mesh):
    in_specs = (
        P(None, "row", None, None, "col", None),
        P("row", "col", None, None, None),
        P("row", "col", None),
        P("row", "col", None),
    )
    out_specs = P(None, "row", None, None, "col", None)
    return jax.shard_map(
        per_device, mesh=mesh, in_specs=in_specs, out_specs=out_specs, check_vma=False
    )
```

profile of v0, /device:TPU:1, one launch (start us, length us, event | category | flops | bytes accessed | tf_op | source)
XLA Modules:
  0.0 712.7 jit_solution(14597959788341730785)
XLA Ops:
  6.5 0.7 multiply_add_fusion.1
  7.2 0.1 fusion.17
  7.3 0.2 reduce_window_sum.11
  7.5 0.2 select_reduce_fusion.1
  7.7 0.7 fusion.26
  8.4 1.0 scatter_custom_fusion.1
  9.3 0.8 all_to_all.10
  10.1 11.5 %all-to-all-start.1 = ((s32[128,2,1]{1,2,0:T(1,128)}), s32[128,2,1]{1,2,0:T(1,128)S(1)}, u32[]{:S(2)}, u32[]{:S(2)}) async-start(s32[128,2,1]{1,2,0:T(1,128)} %bitcast.9), calls=%async_computation.1 | async-start | bytes 131072 | tf_op jit(solution)/shard_map/all_to_all | solution.py:48
  21.6 7.8 %broadcast_in_dim.58 = f32[256,128,128]{2,1,0:T(8,128)} broadcast(f32[]{:T(128)} %constant.112.clone.1), dimensions={} | broadcast | bytes 16777220 | tf_op jit(solution)/shard_map/broadcast_in_dim | solution.py:43
  29.5 23.4 %scatter_fusion = f32[256,128,128]{2,1,0:T(8,128)} fusion(f32[256,128,128]{2,1,0:T(8,128)} %broadcast_in_dim.58, s32[128]{0:T(128)S(1)} %fusion.26, f32[128,128,128]{2,1,0:T(8,128)} %bitcast.97), kind=kCustom, calls=%fused_computation | custom fusion | bytes 25166336 | tf_op jit(solution)/shard_map/scatter | solution.py:43
  52.8 0.0 all-to-all-done.1
  52.8 10.3 %all-to-all-start = ((f32[256,128,128]{2,1,0:T(8,128)}), f32[256,128,128]{2,1,0:T(8,128)}, u32[]{:S(2)}, u32[]{:S(2)}) async-start(f32[256,128,128]{2,1,0:T(8,128)} %scatter_fusion), calls=%async_computation | async-start | bytes 33554432 | tf_op jit(solution)/shard_map/all_to_all | solution.py:47
  63.1 0.2 all-reduce.3.cloned.1.call-start
  63.3 14.1 %copy.25 = f32[48,1,128,2,1,128]{2,5,3,0,4,1:T(8,128)} copy(f32[48,1,128,2,1,128]{5,4,3,2,1,0:T(1,128)} %param.4) | data formatting | bytes 12582912 | tf_op args[0]
  77.4 0.5 broadcast.315
  77.9 0.8 reduce.9
  78.8 0.1 eq.57
  78.9 209.0 %all-to-all-done = f32[256,128,128]{2,1,0:T(8,128)} async-done(((f32[256,128,128]{2,1,0:T(8,128)}), f32[256,128,128]{2,1,0:T(8,128)}, u32[]{:S(2)}, u32[]{:S(2)}) %all-to-all-start) | async-done | bytes 16777248 | tf_op jit(solution)/shard_map/all_to_all | solution.py:47
  287.9 22.8 %fusion = f32[128,128,48,2]{1,2,3,0:T(8,128)} fusion(f32[256,128,128,1]{2,1,0,3:T(8,128)} %bitcast.8, s32[48,2]{0,1:T(2,128)S(1)} %multiply_add_fusion, s32[256]{0:T(256)S(1)} %eq.57), kind=kOutput, calls=%fused_computation.2 | convolution fusion | flops 4831862784 | bytes 23070080 | tf_op jit(solution)/shard_map/ams,spq->apmq/dot_general | solution.py:54
  310.7 6.6 copy.28
  317.3 5.9 bitcast_add_fusion
  323.2 0.0 copy-start
  323.2 2.7 copy-done
  325.9 0.6 fusion.13
  326.6 0.0 all-reduce.3.cloned.1.call-update
  326.6 0.3 all-reduce.5.cloned.1.call-start
  326.9 131.3 %all-reduce.3.cloned.1.call-done = f32[128,128]{0,1:T(8,128)} async-done(((f32[128,128]{0,1:T(8,128)}), f32[128,128]{0,1:T(8,128)}) %all-reduce.3.cloned.1.call-update) | async-done | bytes 65552 | tf_op jit(solution)/shard_map/psum | solution.py:11
  458.2 0.9 copy.29
  459.1 0.9 fusion.16
  460.0 0.1 copy.30
  460.1 11.7 %cholesky.15 = f32[128,128]{1,0:T(8,128)S(1)} custom-call(f32[128,128]{1,0:T(8,128)S(1)} %fusion.15), custom_call_target="Cholesky" | custom-call | tf_op jit(solution)/shard_map/jit(cholesky)/cholesky | solution.py:15
  471.9 0.7 compare_reduce_fusion
  472.6 0.7 fusion.12
  473.3 9.8 %custom-call.7 = f32[1,128,128]{1,2,0:T(8,128)S(1)} custom-call(f32[1,128,128]{2,1,0:T(8,128)S(1)} %fusion.12), custom_call_target="InvertDiagBlocksLowerTriangular" | custom-call | tf_op jit(solution)/shard_map/jit(_solve_triangular)/triangular_solve | solution.py:21
  483.1 7.9 %fusion.7 = f32[48,128,128]{2,1,0:T(8,128)} fusion(f32[48,128,2,128]{1,3,2,0:T(8,128)} %copy-done, pred[]{:T(512)S(6)} %eq.53, f32[1,128,128]{1,2,0:T(8,128)S(1)} %custom-call.7), kind=kOutput, calls=%fused_computation.10 | convolution fusion | flops 1208745984 | bytes 6356993 | tf_op jit(solution)/shard_map/jit(_solve_triangular)/triangular_solve | solution.py:21
  491.0 0.0 all-reduce.5.cloned.1.call-update
  491.0 0.3 all-gather.3.cloned.1.call-start
  491.3 141.6 %all-reduce.5.cloned.1.call-done = f32[48,128,128]{2,1,0:T(8,128)} async-done(((f32[48,128,128]{2,1,0:T(8,128)}), f32[48,128,128]{2,1,0:T(8,128)}) %all-reduce.5.cloned.1.call-update) | async-done | bytes 3145744 | tf_op jit(solution)/shard_map/psum | solution.py:11
  632.9 0.0 copy-start.1
  632.9 1.6 slice.28
  634.5 0.0 all-gather.3.cloned.1.call-update
  634.6 3.7 copy.33
  638.3 44.0 %all-gather.3.cloned.1.call-done = f32[16,128,128]{2,1,0:T(8,128)} async-done(((f32[1,128,128]{2,1,0:T(8,128)}), f32[16,128,128]{2,1,0:T(8,128)}) %all-gather.3.cloned.1.call-update) | async-done | bytes 1048592 | tf_op jit(solution)/shard_map/all_gather | solution.py:62
  682.3 0.0 copy-done.1
  682.3 9.8 %select_bitcast_fusion = f32[48,1,128,2,1,128]{2,5,3,0,4,1:T(8,128)} fusion(f32[48,128,2,128]{1,3,2,0:T(8,128)} %copy-done, f32[48,128,128]{1,2,0:T(8,128)} %copy.33, pred[48]{0:T(512)(128)(4,1)S(1)} %add_compare_fusion, pred[2]{0:T(512)(128)(4,1)S(1)} %add_compare_fusion.1, f32[48,128,128]{2,1,0:T(8,128)S(1)} %copy-done.1, f32[2,8,128,128]{3,2,1,0:T(8,128)} %bitcast.98, ...), kind=kOutput, calls=%fused_computation.5 | convolution fusion | flops 2420637696 | bytes 19005494 | tf_op jit(solution)/shard_map/apk,mqk->apmq/dot_general | solution.py:65
  692.1 14.1 %copy.36 = f32[48,1,128,2,1,128]{5,4,3,2,1,0:T(1,128)} copy(f32[48,1,128,2,1,128]{2,5,3,0,4,1:T(8,128)} %select_bitcast_fusion) | data formatting | bytes 12582912 | tf_op jit(solution)/shard_map/reshape | solution.py:74
  (5 shorter events, 0.1 us)
Async XLA Ops:
  10.1 42.7 %all-to-all-start.1 = ((s32[128,2,1]{1,2,0:T(1,128)}), s32[128,2,1]{1,2,0:T(1,128)S(1)}, u32[]{:S(2)}, u32[]{:S(2)}) async-start(s32[128,2,1]{1,2,0:T(1,128)} %bitcast.9), calls=%async_computation.1 | async-start | bytes 131072 | tf_op jit(solution)/shard_map/all_to_all | solution.py:48
  52.8 235.1 %all-to-all-start = ((f32[256,128,128]{2,1,0:T(8,128)}), f32[256,128,128]{2,1,0:T(8,128)}, u32[]{:S(2)}, u32[]{:S(2)}) async-start(f32[256,128,128]{2,1,0:T(8,128)} %scatter_fusion), calls=%async_computation | async-start | bytes 33554432 | tf_op jit(solution)/shard_map/all_to_all | solution.py:47
  63.1 395.1 %all-reduce.3.cloned.1.call-start = ((), (), s32[]{:S(2)}) async-start(), calls=%async_computation.2 | async-start | bytes 131072 | tf_op jit(solution)/shard_map/psum | solution.py:11
  323.2 2.7 copy-start
  326.6 306.3 %all-reduce.5.cloned.1.call-start = ((), (), s32[]{:S(2)}) async-start(), calls=%async_computation.3 | async-start | bytes 6291456 | tf_op jit(solution)/shard_map/psum | solution.py:11
  491.0 191.3 %all-gather.3.cloned.1.call-start = ((), (), s32[]{:S(2)}) async-start(), calls=%async_computation.4 | async-start | bytes 1114112 | tf_op jit(solution)/shard_map/all_gather | solution.py:62
  632.9 49.3 %copy-start.1 = (f32[48,128,128]{2,1,0:T(8,128)S(1)}, f32[48,128,128]{2,1,0:T(8,128)}, u32[]{:S(2)}) copy-start(f32[48,128,128]{2,1,0:T(8,128)} %all-reduce.5.cloned.1.call-done) | copy-start | bytes 9437188
Sparse Core Ops, SparseCore 0:
  326.7 131.4 all-reduce.2
  491.1 141.7 all-reduce.4
  635.6 46.6 all-gather.2
where the time goes:
time: 714 us; the launch traced here: 713 us
  waiting for transfers between devices  526 us (74%)
  local copies, waits for them, and re-layouts  77.4 us (11%)
  matrix products  40.4 us (6%)
  other arithmetic  33 us (5%)
  starting transfers between devices  22.6 us (3%)
  between operations  13.2 us (2%)
    psum x2, waiting for transfers between devices, broadcast(): return lax.psum(kept, axis)  273 us
    all_to_all x1, waiting for transfers between devices, per_device(): lax.all_to_all(send_tiles, ('row', 'col'), split_axis=0, concat_axis=0, t...  209 us
    all_gather x1, waiting for transfers between devices, per_device(): lax.all_gather(panel_rows[:window_blocks][:, None], 'row', axis=1, tiled=...  44 us
    scatter x1, local copies, waits for them, and re-layouts, per_device(): jnp.zeros((slot_total, tile_size, tile_size), jnp.float32).at[send_slot]  23.4 us
    dot_general x1, matrix products, per_device(): jnp.einsum('ams,spq->apmq', selector, arrived_tiles, precision=lax.Precis...  22.8 us
    unnamed x5, local copies, waits for them, and re-layouts  16.8 us
  transfers between devices with their start and end apart: 5, of which 4 were waited for; matrix products, arithmetic and copies ran while one was open for 7% of the time, Pallas kernels for 0%

commit v1 on v0

--- a/solution.py
+++ b/solution.py
@@ -59,7 +59,12 @@
     panel_rows = solve_panel(factor_of(corner), column)
     panel_rows = broadcast(panel_rows, "col", 0)
     window_blocks = col_blocks * col_count // row_count
-    window = lax.all_gather(panel_rows[:window_blocks][:, None], "row", axis=1, tiled=True)
+    window = jnp.concatenate(
+        lax.all_to_all(
+            jnp.stack([panel_rows[:window_blocks][:, None]] * lax.axis_size("row")), "row", 0, 0
+        ),
+        axis=1,
+    )
     window = window.reshape(col_blocks, col_count, tile_size, tile_size)
     own_window = lax.dynamic_index_in_dim(window, col_index, axis=1, keepdims=False)
     update = jnp.einsum("apk,mqk->apmq", panel_rows, own_window, precision=lax.Precision.HIGHEST)

time: 714 us -> 692 us (0.969)
  waiting for transfers between devices: 526 us -> 496 us
  starting transfers between devices: 22.6 us -> 30.2 us
    all_gather x1 -> x0, waiting for transfers between devices: 44 us -> none  [per_device(): lax.all_gather(panel_rows[:window_blocks][:, None], 'row', axis=1, tiled=...]
    all_to_all x0 -> x1, waiting for transfers between devices: none -> 13.7 us  [per_device(): lax.all_to_all(jnp.stack([panel_rows[:window_blocks][:, None]] * lax.axis...]
    all_to_all x0 -> x1, starting transfers between devices: none -> 7.98 us  [per_device(): lax.all_to_all(jnp.stack([panel_rows[:window_blocks][:, None]] * lax.axis...]
where the time goes in v1:
time: 692 us; the launch traced here: 691 us
  waiting for transfers between devices  496 us (72%)
  local copies, waits for them, and re-layouts  77.8 us (11%)
  matrix products  40.4 us (6%)
  other arithmetic  33 us (5%)
  starting transfers between devices  30.2 us (4%)
  between operations  13.5 us (2%)
    psum x2, waiting for transfers between devices, broadcast(): return lax.psum(kept, axis)  273 us
    all_to_all x1, waiting for transfers between devices, per_device(): lax.all_to_all(send_tiles, ('row', 'col'), split_axis=0, concat_axis=0, t...  209 us
    scatter x1, local copies, waits for them, and re-layouts, per_device(): jnp.zeros((slot_total, tile_size, tile_size), jnp.float32).at[send_slot]  23.4 us
    dot_general x1, matrix products, per_device(): jnp.einsum('ams,spq->apmq', selector, arrived_tiles, precision=lax.Precis...  22.8 us
    unnamed x5, local copies, waits for them, and re-layouts  16.8 us
    reshape x1, local copies, waits for them, and re-layouts, per_device(): return result.reshape(front.shape)  14.1 us
  transfers between devices with their start and end apart: 5, of which 4 were waited for; matrix products, arithmetic and copies ran while one was open for 7% of the time, Pallas kernels for 0%

profile of v1, /device:TPU:1, one launch (start us, length us, event | category | flops | bytes accessed | tf_op | source)
XLA Modules:
  0.0 691.0 jit_solution(2936056699891731385)
XLA Ops:
  6.5 0.7 multiply_add_fusion.1
  7.2 0.1 fusion.17
  7.3 0.2 reduce_window_sum.11
  7.5 0.2 select_reduce_fusion.1
  7.7 0.7 fusion.26
  8.4 1.0 scatter_custom_fusion.1
  9.3 0.8 all_to_all.13
  10.1 11.5 %all-to-all-start.1 = ((s32[128,2,1]{1,2,0:T(1,128)}), s32[128,2,1]{1,2,0:T(1,128)S(1)}, u32[]{:S(2)}, u32[]{:S(2)}) async-start(s32[128,2,1]{1,2,0:T(1,128)} %bitcast.9), calls=%async_computation.1 | async-start | bytes 131072 | tf_op jit(solution)/shard_map/all_to_all | solution.py:48
  21.6 7.8 %broadcast_in_dim.55 = f32[256,128,128]{2,1,0:T(8,128)} broadcast(f32[]{:T(128)} %constant.112.clone.1), dimensions={} | broadcast | bytes 16777220 | tf_op jit(solution)/shard_map/broadcast_in_dim | solution.py:43
  29.5 23.4 %scatter_fusion = f32[256,128,128]{2,1,0:T(8,128)} fusion(f32[256,128,128]{2,1,0:T(8,128)} %broadcast_in_dim.55, s32[128]{0:T(128)S(1)} %fusion.26, f32[128,128,128]{2,1,0:T(8,128)} %bitcast.97), kind=kCustom, calls=%fused_computation | custom fusion | bytes 25166336 | tf_op jit(solution)/shard_map/scatter | solution.py:43
  52.8 0.0 all-to-all-done.1
  52.8 10.3 %all-to-all-start = ((f32[256,128,128]{2,1,0:T(8,128)}), f32[256,128,128]{2,1,0:T(8,128)}, u32[]{:S(2)}, u32[]{:S(2)}) async-start(f32[256,128,128]{2,1,0:T(8,128)} %scatter_fusion), calls=%async_computation | async-start | bytes 33554432 | tf_op jit(solution)/shard_map/all_to_all | solution.py:47
  63.1 0.2 all-reduce.3.cloned.1.call-start
  63.3 14.1 %copy.25 = f32[48,1,128,2,1,128]{2,5,3,0,4,1:T(8,128)} copy(f32[48,1,128,2,1,128]{5,4,3,2,1,0:T(1,128)} %param.4) | data formatting | bytes 12582912 | tf_op args[0]
  77.4 0.5 broadcast.318
  77.9 0.8 reduce.9
  78.8 0.1 eq.57
  78.9 209.0 %all-to-all-done = f32[256,128,128]{2,1,0:T(8,128)} async-done(((f32[256,128,128]{2,1,0:T(8,128)}), f32[256,128,128]{2,1,0:T(8,128)}, u32[]{:S(2)}, u32[]{:S(2)}) %all-to-all-start) | async-done | bytes 16777248 | tf_op jit(solution)/shard_map/all_to_all | solution.py:47
  287.9 22.8 %fusion = f32[128,128,48,2]{1,2,3,0:T(8,128)} fusion(f32[256,128,128,1]{2,1,0,3:T(8,128)} %bitcast.8, s32[48,2]{0,1:T(2,128)S(1)} %multiply_add_fusion, s32[256]{0:T(256)S(1)} %eq.57), kind=kOutput, calls=%fused_computation.2 | convolution fusion | flops 4831862784 | bytes 23070080 | tf_op jit(solution)/shard_map/ams,spq->apmq/dot_general | solution.py:54
  310.7 6.6 copy.28
  317.3 5.9 bitcast_add_fusion
  323.2 0.0 copy-start
  323.2 2.7 copy-done
  325.9 0.6 fusion.13
  326.6 0.0 all-reduce.3.cloned.1.call-update
  326.6 0.3 all-reduce.5.cloned.1.call-start
  326.9 131.3 %all-reduce.3.cloned.1.call-done = f32[128,128]{0,1:T(8,128)} async-done(((f32[128,128]{0,1:T(8,128)}), f32[128,128]{0,1:T(8,128)}) %all-reduce.3.cloned.1.call-update) | async-done | bytes 65552 | tf_op jit(solution)/shard_map/psum | solution.py:11
  458.2 0.9 copy.29
  459.1 0.9 fusion.16
  460.0 0.1 copy.30
  460.1 11.7 %cholesky.15 = f32[128,128]{1,0:T(8,128)S(1)} custom-call(f32[128,128]{1,0:T(8,128)S(1)} %fusion.15), custom_call_target="Cholesky" | custom-call | tf_op jit(solution)/shard_map/jit(cholesky)/cholesky | solution.py:15
  471.9 0.7 compare_reduce_fusion
  472.6 0.7 fusion.12
  473.3 9.8 %custom-call.7 = f32[1,128,128]{1,2,0:T(8,128)S(1)} custom-call(f32[1,128,128]{2,1,0:T(8,128)S(1)} %fusion.12), custom_call_target="InvertDiagBlocksLowerTriangular" | custom-call | tf_op jit(solution)/shard_map/jit(_solve_triangular)/triangular_solve | solution.py:21
  483.1 7.9 %fusion.7 = f32[48,128,128]{2,1,0:T(8,128)} fusion(f32[48,128,2,128]{1,3,2,0:T(8,128)} %copy-done, pred[]{:T(512)S(6)} %eq.53, f32[1,128,128]{1,2,0:T(8,128)S(1)} %custom-call.7), kind=kOutput, calls=%fused_computation.10 | convolution fusion | flops 1208745984 | bytes 6356993 | tf_op jit(solution)/shard_map/jit(_solve_triangular)/triangular_solve | solution.py:21
  491.0 0.0 all-reduce.5.cloned.1.call-update
  491.0 142.0 %all-reduce.5.cloned.1.call-done = f32[48,128,128]{2,1,0:T(8,128)} async-done(((f32[48,128,128]{2,1,0:T(8,128)}), f32[48,128,128]{2,1,0:T(8,128)}) %all-reduce.5.cloned.1.call-update) | async-done | bytes 3145744 | tf_op jit(solution)/shard_map/psum | solution.py:11
  632.9 0.0 copy-start.1
  632.9 1.0 slice_bitcast_fusion.4
  633.9 1.1 stack.3
  635.0 8.0 %all-to-all-start.2 = ((f32[16,1,1,128,128]{4,3,2,1,0:T(8,128)}), f32[16,1,1,128,128]{4,3,2,1,0:T(8,128)}, u32[]{:S(2)}, u32[]{:S(2)}) async-start(f32[16,1,1,128,128]{4,3,2,1,0:T(8,128)} %stack.3), calls=%async_computation.2 | async-start | bytes 2097152 | tf_op jit(solution)/shard_map/all_to_all | solution.py:63
  643.0 3.6 copy.33
  646.6 13.7 %all-to-all-done.2 = f32[16,1,1,128,128]{4,3,2,1,0:T(8,128)} async-done(((f32[16,1,1,128,128]{4,3,2,1,0:T(8,128)}), f32[16,1,1,128,128]{4,3,2,1,0:T(8,128)}, u32[]{:S(2)}, u32[]{:S(2)}) %all-to-all-start.2) | async-done | bytes 1048608 | tf_op jit(solution)/shard_map/all_to_all | solution.py:63
  660.3 0.0 copy-done.1
  660.3 9.8 %select_bitcast_fusion = f32[48,1,128,2,1,128]{2,5,3,0,4,1:T(8,128)} fusion(f32[48,128,2,128]{1,3,2,0:T(8,128)} %copy-done, f32[48,128,128]{1,2,0:T(8,128)} %copy.33, pred[48]{0:T(512)(128)(4,1)S(1)} %add_compare_fusion, pred[2]{0:T(512)(128)(4,1)S(1)} %add_compare_fusion.1, f32[48,128,128]{2,1,0:T(8,128)S(1)} %copy-done.1, f32[2,8,128,128]{3,2,1,0:T(8,128)} %bitcast.22, ...), kind=kOutput, calls=%fused_computation.5 | convolution fusion | flops 2420637696 | bytes 19005494 | tf_op jit(solution)/shard_map/apk,mqk->apmq/dot_general | solution.py:70
  670.1 14.1 %copy.35 = f32[48,1,128,2,1,128]{5,4,3,2,1,0:T(1,128)} copy(f32[48,1,128,2,1,128]{2,5,3,0,4,1:T(8,128)} %select_bitcast_fusion) | data formatting | bytes 12582912 | tf_op jit(solution)/shard_map/reshape | solution.py:79
  (5 shorter events, 0.1 us)
Async XLA Ops:
  10.1 42.7 %all-to-all-start.1 = ((s32[128,2,1]{1,2,0:T(1,128)}), s32[128,2,1]{1,2,0:T(1,128)S(1)}, u32[]{:S(2)}, u32[]{:S(2)}) async-start(s32[128,2,1]{1,2,0:T(1,128)} %bitcast.9), calls=%async_computation.1 | async-start | bytes 131072 | tf_op jit(solution)/shard_map/all_to_all | solution.py:48
  52.8 235.1 %all-to-all-start = ((f32[256,128,128]{2,1,0:T(8,128)}), f32[256,128,128]{2,1,0:T(8,128)}, u32[]{:S(2)}, u32[]{:S(2)}) async-start(f32[256,128,128]{2,1,0:T(8,128)} %scatter_fusion), calls=%async_computation | async-start | bytes 33554432 | tf_op jit(solution)/shard_map/all_to_all | solution.py:47
  63.1 395.1 %all-reduce.3.cloned.1.call-start = ((), (), s32[]{:S(2)}) async-start(), calls=%async_computation.3 | async-start | bytes 131072 | tf_op jit(solution)/shard_map/psum | solution.py:11
  323.2 2.7 copy-start
  326.6 306.3 %all-reduce.5.cloned.1.call-start = ((), (), s32[]{:S(2)}) async-start(), calls=%async_computation.4 | async-start | bytes 6291456 | tf_op jit(solution)/shard_map/psum | solution.py:11
  632.9 27.4 %copy-start.1 = (f32[48,128,128]{2,1,0:T(8,128)S(1)}, f32[48,128,128]{2,1,0:T(8,128)}, u32[]{:S(2)}) copy-start(f32[48,128,128]{2,1,0:T(8,128)} %all-reduce.5.cloned.1.call-done) | copy-start | bytes 9437188
  635.0 25.3 %all-to-all-start.2 = ((f32[16,1,1,128,128]{4,3,2,1,0:T(8,128)}), f32[16,1,1,128,128]{4,3,2,1,0:T(8,128)}, u32[]{:S(2)}, u32[]{:S(2)}) async-start(f32[16,1,1,128,128]{4,3,2,1,0:T(8,128)} %stack.3), calls=%async_computation.2 | async-start | bytes 2097152 | tf_op jit(solution)/shard_map/all_to_all | solution.py:63
Sparse Core Ops, SparseCore 0:
  326.7 131.4 all-reduce.2
  491.1 141.7 all-reduce.4
